TPU v7x, 512 devices: a whole 4x4x16 slice. The times are simulated.
512 devices in a mesh: row: 16 (over y, x), col: 32 (over z, core).
Axes of the slice: x: 4, y: 4, z: 16, core: 2. Of those that a mesh axis runs over, the one named last changes fastest.
Arguments:
- points: bfloat16 [262144, 256], P(('col', 'row')), may hold values from -6 to 6
- weights: bfloat16 [262144, 128], P(('col', 'row')), may hold values from -6 to 6
- near_blocks: int32 [2048, 16], P(('col', 'row')), may hold values from 0 to 2047, as said below
- proxies: bfloat16 [64, 256], replicated, may hold values from -6 to 6
Outputs:
- near_product: bfloat16 [262144, 128], P(('col', 'row'))
- factors: float32 [32768, 192], P(('col', 'row'))
Inputs may be any that keep to these rules, and one draw needn't show every extreme that they name: near_blocks[j, 0] = j; every entry of row j lies in the column group of j, that is in the same run of 64 blocks; entries may repeat.
All inputs are finite; a program needn't handle non-finite values.
Results may differ from a plain program's by a relative error of at most 0.01.
Values may be sent and summed in bfloat16 or wider, within the bound.
No kernel may reach another device: no remote copies, remote signals or barrier semaphores. Data moves between devices by JAX's collectives and lax.ppermute only.
A program may use at most 64 MiB of HBM per device.

v0:
```python
import jax
import jax.numpy as jnp
from jax import lax
from jax.sharding import PartitionSpec as P

DIM = 256
BLK = 128
NV = 128


def partner(value, axis, stride):
    mask = 2**stride
    pairs = [(source, source ^ mask) for source in range(lax.axis_size(axis))]
    return lax.ppermute(value, axis, pairs)


def kern_tile(left, right):
    cross = jnp.dot(left, right.T, preferred_element_type=jnp.float32)
    lnorm = jnp.sum(left.astype(jnp.float32) ** 2, axis=-1)
    rnorm = jnp.sum(right.astype(jnp.float32) ** 2, axis=-1)
    return jnp.exp(-(lnorm[:, None] + rnorm[None, :] - 2.0 * cross) * (2.0 / DIM))


def level_merge(lower_own, lower_other):
    high = lax.Precision.HIGHEST
    gram = jnp.dot(lower_own, lower_own.T, precision=high) + jnp.dot(
        lower_other, lower_other.T, precision=high
    )
    merged = jnp.linalg.cholesky(gram)
    transfer = lax.linalg.triangular_solve(merged, lower_own, left_side=True, lower=True).T
    return (merged, transfer)


def on_device(points, weights, near_blocks, proxies):
    n_local = near_blocks.shape[0]
    group_count = n_local * lax.axis_size("row")
    base = lax.axis_index("col") * group_count
    gathered = lax.all_gather(points, "row", axis=0, tiled=True)
    tblocks = gathered.reshape(group_count, BLK, DIM)
    local_ids = near_blocks - base
    sources = points.reshape(n_local, BLK, DIM)
    wblocks = weights.reshape(n_local, BLK, NV)
    targets = tblocks[local_ids]
    cross = jnp.einsum("jtad,jbd->jtab", targets, sources, preferred_element_type=jnp.float32)
    tnorm = jnp.sum(targets.astype(jnp.float32) ** 2, axis=-1)
    snorm = jnp.sum(sources.astype(jnp.float32) ** 2, axis=-1)
    dist = tnorm[:, :, :, None] + snorm[:, None, None, :] - 2.0 * cross
    tile = jnp.exp(-dist * (2.0 / DIM)).astype(jnp.bfloat16)
    contrib = jnp.einsum("jtab,jbv->jtav", tile, wblocks, preferred_element_type=jnp.float32)
    partial_value = jnp.zeros((group_count, BLK, NV), jnp.float32)
    partial_value = partial_value.at[local_ids.reshape(-1)].add(contrib.reshape(-1, BLK, NV))
    near_sum = lax.psum_scatter(
        partial_value.reshape(group_count * BLK, NV), "row", scatter_dimension=0, tiled=True
    )
    near_product = near_sum.astype(jnp.bfloat16)
    far = kern_tile(points, proxies)
    lower0 = jnp.linalg.cholesky(jnp.dot(far.T, far, precision=lax.Precision.HIGHEST))
    current = lower0
    transfers = []
    for level in range(2):
        sibling = partner(current, "col", level)
        current, transfer = level_merge(current, sibling)
        transfers.append(transfer)
    factors = jnp.concatenate([transfers[0], transfers[1], current.T], axis=1)
    return (near_product, factors)


def solution(mesh):
    placed = (P(("col", "row"), None), P(("col", "row"), None), P(("col", "row"), None), P())
    return jax.shard_map(
        on_device,
        mesh=mesh,
        in_specs=placed,
        out_specs=(P(("col", "row"), None), P(("col", "row"), None)),
        check_vma=False,
    )
```

profile of v0, /device:TPU:2, one launch (start us, length us, event | category | flops | bytes accessed | tf_op | source)
XLA Modules:
  0.0 213.1 jit_solution(5560618731934013219)
XLA Ops:
  7.2 0.7 all-gather.2.cloned.1.call-update
  8.0 0.7 compare_select_fusion
  8.8 1.1 multiply_reduce_fusion.1
  9.9 72.4 %all-gather.2.cloned.1.call-done = bf16[8192,256]{1,0:T(8,128)(2,1)} async-done(((bf16[512,256]{1,0:T(8,128)(2,1)}), bf16[8192,256]{1,0:T(8,128)(2,1)}) %all-gather.2.cloned.1.call-update) | async-done | bytes 4194320 | tf_op jit(solution)/shard_map/all_gather | solution.py:38
  82.4 5.0 %gather_fusion = bf16[64,128,256]{2,1,0:T(8,128)(2,1)} fusion(bf16[64,128,256]{2,1,0:T(8,128)(2,1)} %bitcast.66, s32[1024]{0:T(1024)S(1)} %pad_clamp_fusion), kind=kCustom, calls=%fused_computation | custom fusion | bytes 8388864 | tf_op jit(solution)/shard_map/gather | solution.py:43
  87.3 3.4 %multiply_reduce_fusion = f32[4,16,128]{2,1,0:T(8,128)S(1)} fusion(bf16[4,16,128,256]{3,2,1,0:T(8,128)(2,1)} %bitcast.64), kind=kLoop, calls=%fused_computation.2 | loop fusion | flops 6283264 | bytes 4227072 | tf_op jit(solution)/shard_map/reduce_sum | solution.py:45
  90.7 4.9 %fusion = f32[4,16,128,128]{3,2,1,0:T(8,128)} fusion(bf16[4,128,128,1]{2,1,3,0:T(8,128)(2,1)S(1)} %bitcast.62, bf16[4,16,128,256]{3,2,1,0:T(8,128)(2,1)} %bitcast.65, bf16[4,128,256,1]{2,1,3,0:T(8,128)(2,1)S(1)} %bitcast.68, f32[4,128]{1,0:T(4,128)S(1)} %bitcast.69, f32[4,16,128]{2,1,0:T(8,128)S(1)} %multiply_reduce_fusion), kind=kOutput, calls=%fused_computation.4 | convolution fusion | flops 811597824 | bytes 8816640 | tf_op jit(solution)/shard_map/jtab,jbv->jtav/dot_general | solution.py:49
  95.6 2.5 %broadcast_in_dim.4 = f32[64,128,128]{2,1,0:T(8,128)} broadcast(f32[]{:T(128)} %constant.43.clone.1), dimensions={} | broadcast | bytes 4194308 | tf_op jit(solution)/shard_map/broadcast_in_dim | solution.py:50
  98.1 13.6 %scatter_fusion = f32[64,128,128]{2,1,0:T(8,128)} fusion(f32[64,128,128]{2,1,0:T(8,128)} %broadcast_in_dim.4, s32[64]{0:T(128)S(1)} %fusion.15, f32[64,128,128]{2,1,0:T(8,128)} %bitcast.67), kind=kCustom, calls=%fused_computation.1 | custom fusion | flops 1048576 | bytes 12583168 | tf_op jit(solution)/shard_map/scatter-add | solution.py:51
  111.8 0.7 copy-done.2
  113.6 5.8 %cholesky.59 = f32[64,64]{1,0:T(8,128)S(1)} custom-call(f32[64,64]{1,0:T(8,128)S(1)} %fusion.9), custom_call_target="Cholesky" | custom-call | tf_op jit(solution)/shard_map/jit(cholesky)/cholesky | solution.py:57
  120.1 0.7 fusion.10
  120.8 1.9 collective-permute-start
  122.9 1.0 collective-permute-done
  124.2 5.8 %cholesky.70 = f32[64,64]{1,0:T(8,128)S(1)} custom-call(f32[64,64]{1,0:T(8,128)S(1)} %fusion.8), custom_call_target="Cholesky" | custom-call | tf_op jit(solution)/shard_map/jit(cholesky)/cholesky | solution.py:29
  130.7 0.7 select_bitcast_fusion.1
  131.3 3.3 %collective-permute-start.1 = (f32[64,64]{1,0:T(8,128)S(1)}, f32[64,64]{1,0:T(8,128)S(1)}, u32[]{:S(2)}, u32[]{:S(2)}) collective-permute-start(f32[64,64]{1,0:T(8,128)S(1)} %get-tuple-element.7), channel_id=1, source_target_pairs={{0,2},{1,3},{2,0},{3,1},{4,6},{5,7},{6,4},{7,5},{8,10},{9,11},{10,... | collective-permute-start | bytes 49160 | tf_op jit(solution)/shard_map/ppermute | solution.py:14
  134.7 4.9 %custom-call.6 = f32[1,64,64]{1,2,0:T(8,128)S(1)} custom-call(f32[1,64,64]{2,1,0:T(8,128)S(1)} %get-tuple-element.6), custom_call_target="InvertDiagBlocksLowerTriangular" | custom-call | tf_op jit(solution)/shard_map/triangular_solve/custom-call.0 | solution.py:30
  140.3 5.8 %cholesky.81 = f32[64,64]{1,0:T(8,128)S(1)} custom-call(f32[64,64]{1,0:T(8,128)S(1)} %fusion.6), custom_call_target="Cholesky" | custom-call | tf_op jit(solution)/shard_map/jit(cholesky)/cholesky | solution.py:29
  146.8 0.7 select_bitcast_fusion
  147.5 4.9 %custom-call.7 = f32[1,64,64]{1,2,0:T(8,128)S(1)} custom-call(f32[1,64,64]{2,1,0:T(8,128)S(1)} %get-tuple-element.10), custom_call_target="InvertDiagBlocksLowerTriangular" | custom-call | tf_op jit(solution)/shard_map/triangular_solve/custom-call.0 | solution.py:30
  152.7 0.7 copy.15
  153.4 51.3 %reduce-scatter.2.cloned.1.call-done = f32[512,128]{1,0:T(8,128)} async-done(((f32[8192,128]{1,0:T(8,128)}), f32[512,128]{1,0:T(8,128)}) %reduce-scatter.2.cloned.1.call-update) | async-done | bytes 262160 | tf_op jit(solution)/shard_map/reduce_scatter | solution.py:52
  204.7 1.6 convert_element_type.20
  (35 shorter events, 4.7 us)
Async XLA Ops:
  7.2 83.6 %copy-start = (bf16[512,128]{1,0:T(8,128)(2,1)S(1)}, bf16[512,128]{1,0:T(8,128)(2,1)}, u32[]{:S(2)}) copy-start(bf16[512,128]{1,0:T(8,128)(2,1)} %param.8) | copy-start | bytes 393220
  7.2 75.2 %all-gather.2.cloned.1.call-start = ((), (), s32[]{:S(2)}) async-start(), calls=%async_computation.1 | async-start | bytes 4456448 | tf_op jit(solution)/shard_map/all_gather | solution.py:38
  7.9 196.8 %reduce-scatter.2.cloned.1.call-start = ((), (), s32[]{:S(2)}) async-start(), calls=%async_computation.2 | async-start | bytes 4456448 | tf_op jit(solution)/shard_map/reduce_scatter | solution.py:52
  87.3 3.4 %copy-start.1 = (bf16[512,256]{1,0:T(8,128)(2,1)S(1)}, bf16[512,256]{1,0:T(8,128)(2,1)}, u32[]{:S(2)}) copy-start(bf16[512,256]{1,0:T(8,128)(2,1)} %param.7) | copy-start | bytes 786436
  111.8 0.8 copy-start.2
  120.8 3.1 %collective-permute-start = (f32[64,64]{1,0:T(8,128)S(1)}, f32[64,64]{1,0:T(8,128)S(1)}, u32[]{:S(2)}, u32[]{:S(2)}) collective-permute-start(f32[64,64]{1,0:T(8,128)S(1)} %fusion.10), channel_id=1, source_target_pairs={{0,1},{1,0},{2,3},{3,2},{4,5},{5,4},{6,7},{7,6},{8,9},{9,8},{10,11... | collective-permute-start | bytes 49160 | tf_op jit(solution)/shard_map/ppermute | solution.py:14
  131.3 8.7 %collective-permute-start.1 = (f32[64,64]{1,0:T(8,128)S(1)}, f32[64,64]{1,0:T(8,128)S(1)}, u32[]{:S(2)}, u32[]{:S(2)}) collective-permute-start(f32[64,64]{1,0:T(8,128)S(1)} %get-tuple-element.7), channel_id=1, source_target_pairs={{0,2},{1,3},{2,0},{3,1},{4,6},{5,7},{6,4},{7,5},{8,10},{9,11},{10,... | collective-permute-start | bytes 49160 | tf_op jit(solution)/shard_map/ppermute | solution.py:14
Sparse Core Ops, SparseCore 0:
  11.0 71.2 all-gather.1
  111.9 92.7 reduce-scatter.1
where the time goes:
time: 214 us; the launch traced here: 213 us
  waiting for transfers between devices  125 us (58%)
  other arithmetic  51.9 us (24%)
  between operations  14.3 us (7%)
  local copies, waits for them, and re-layouts  9.3 us (4%)
  matrix products  6.97 us (3%)
  starting transfers between devices  5.31 us (2%)
    all_gather x1, waiting for transfers between devices, on_device(): gathered = lax.all_gather(points, 'row', axis=0, tiled=True)  72.4 us
    reduce_scatter x1, waiting for transfers between devices, on_device(): lax.psum_scatter(partial_value.reshape(group_count * BLK, NV), 'row', sca...  51.3 us
    scatter-add x1, other arithmetic, on_device(): partial_value.at[local_ids.reshape(-1)].add(contrib.reshape(-1, BLK, NV))  13.6 us
    another operation x6, other arithmetic, level_merge(): merged = jnp.linalg.cholesky(gram)  13 us
    another operation x4, other arithmetic, level_merge(): lax.linalg.triangular_solve(merged, lower_own, left_side=True, lower=True)  11.1 us
    another operation x3, other arithmetic, on_device(): jnp.linalg.cholesky(jnp.dot(far.T, far, precision=lax.Precision.HIGHEST))  6.52 us
    ppermute x2, starting transfers between devices, partner(): return lax.ppermute(value, axis, pairs)  5.24 us
    gather x1, local copies, waits for them, and re-layouts, on_device(): targets = tblocks[local_ids]  4.97 us
  transfers between devices with their start and end apart: 4, of which 3 were waited for; matrix products, arithmetic and copies ran while one was open for 17% of the time, Pallas kernels for 0%

commit v1 on v0

--- a/solution.py
+++ b/solution.py
@@ -35,7 +35,9 @@
     n_local = near_blocks.shape[0]
     group_count = n_local * lax.axis_size("row")
     base = lax.axis_index("col") * group_count
-    gathered = lax.all_gather(points, "row", axis=0, tiled=True)
+    gathered = jnp.concatenate(
+        lax.all_to_all(jnp.stack([points] * lax.axis_size("row")), "row", 0, 0), axis=0
+    )
     tblocks = gathered.reshape(group_count, BLK, DIM)
     local_ids = near_blocks - base
     sources = points.reshape(n_local, BLK, DIM)

time: 214 us -> 214 us (level)
  waiting for transfers between devices: 125 us -> 109 us
  starting transfers between devices: 5.31 us -> 21 us
  local copies, waits for them, and re-layouts: 9.3 us -> 12.7 us
    all_gather x1 -> x0, waiting for transfers between devices: 72.4 us -> none  [on_device(): gathered = lax.all_gather(points, 'row', axis=0, tiled=True)]
    all_to_all x0 -> x1, waiting for transfers between devices: none -> 50.9 us  [on_device(): lax.all_to_all(jnp.stack([points] * lax.axis_size('row')), 'row', 0, 0)]
    all_to_all x0 -> x1, starting transfers between devices: none -> 10.3 us  [on_device(): lax.all_to_all(jnp.stack([points] * lax.axis_size('row')), 'row', 0, 0)]
    reduce_scatter x1, waiting for transfers between devices: 51.3 us -> 56.8 us  [on_device(): lax.psum_scatter(partial_value.reshape(group_count * BLK, NV), 'row', sca...]
    ppermute x2, starting transfers between devices: 5.24 us -> 10.7 us  [partner(): return lax.ppermute(value, axis, pairs)]
    another operation x0 -> x1, local copies, waits for them, and re-layouts: none -> 3.36 us  [on_device(): jnp.stack([points] * lax.axis_size('row'))]
  transfers between devices with their start and end apart: 4 -> 4, of which waited for: 3 -> 3; matrix products, arithmetic and copies ran while one was open for 17% -> 16% of each run, Pallas kernels for 0% -> 0%
where the time goes in v1:
time: 214 us
  waiting for transfers between devices  109 us (51%)
  other arithmetic  50.2 us (23%)
  starting transfers between devices  21 us (10%)
  between operations  14.3 us (7%)
  local copies, waits for them, and re-layouts  12.7 us (6%)
  matrix products  6.97 us (3%)
    reduce_scatter x1, waiting for transfers between devices, on_device(): lax.psum_scatter(partial_value.reshape(group_count * BLK, NV), 'row', sca...  56.8 us
    all_to_all x1, waiting for transfers between devices, on_device(): lax.all_to_all(jnp.stack([points] * lax.axis_size('row')), 'row', 0, 0)  50.9 us
    scatter-add x1, other arithmetic, on_device(): partial_value.at[local_ids.reshape(-1)].add(contrib.reshape(-1, BLK, NV))  13.6 us
    another operation x6, other arithmetic, level_merge(): merged = jnp.linalg.cholesky(gram)  13 us
    another operation x4, other arithmetic, level_merge(): lax.linalg.triangular_solve(merged, lower_own, left_side=True, lower=True)  11.1 us
    ppermute x2, starting transfers between devices, partner(): return lax.ppermute(value, axis, pairs)  10.7 us
    all_to_all x1, starting transfers between devices, on_device(): lax.all_to_all(jnp.stack([points] * lax.axis_size('row')), 'row', 0, 0)  10.3 us
    another operation x3, other arithmetic, on_device(): jnp.linalg.cholesky(jnp.dot(far.T, far, precision=lax.Precision.HIGHEST))  6.52 us
  transfers between devices with their start and end apart: 4, of which 3 were waited for; matrix products, arithmetic and copies ran while one was open for 16% of the time, Pallas kernels for 0%

profile of v1, /device:TPU:2, one launch (start us, length us, event | category | flops | bytes accessed | tf_op | source)
XLA Modules:
  0.0 213.8 jit_solution(10297023917232793025)
XLA Ops:
  7.2 3.4 %stack.2 = bf16[16,512,256]{2,1,0:T(8,128)(2,1)} broadcast(bf16[512,256]{1,0:T(8,128)(2,1)} %param.7), dimensions={1,2} | broadcast | bytes 4456448 | tf_op jit(solution)/shard_map/stack | solution.py:39
  10.5 10.3 %all-to-all-start = ((bf16[16,512,256]{2,1,0:T(8,128)(2,1)}), bf16[16,512,256]{2,1,0:T(8,128)(2,1)}, u32[]{:S(2)}, u32[]{:S(2)}) async-start(bf16[16,512,256]{2,1,0:T(8,128)(2,1)} %stack.2), calls=%async_computation | async-start | bytes 8388608 | tf_op jit(solution)/shard_map/all_to_all | solution.py:39
  21.3 50.9 %all-to-all-done = bf16[16,512,256]{2,1,0:T(8,128)(2,1)} async-done(((bf16[16,512,256]{2,1,0:T(8,128)(2,1)}), bf16[16,512,256]{2,1,0:T(8,128)(2,1)}, u32[]{:S(2)}, u32[]{:S(2)}) %all-to-all-start) | async-done | bytes 4194336 | tf_op jit(solution)/shard_map/all_to_all | solution.py:39
  72.2 5.0 %gather_fusion = bf16[64,128,256]{2,1,0:T(8,128)(2,1)} fusion(bf16[64,128,256]{2,1,0:T(8,128)(2,1)} %bitcast.1, s32[1024]{0:T(1024)S(1)} %pad_clamp_fusion), kind=kCustom, calls=%fused_computation | custom fusion | bytes 8388864 | tf_op jit(solution)/shard_map/gather | solution.py:45
  77.2 3.3 %multiply_reduce_fusion = f32[4,16,128]{2,1,0:T(8,128)S(1)} fusion(bf16[4,16,128,256]{3,2,1,0:T(8,128)(2,1)} %bitcast.64), kind=kLoop, calls=%fused_computation.2 | loop fusion | flops 6283264 | bytes 4227072 | tf_op jit(solution)/shard_map/reduce_sum | solution.py:47
  80.5 4.9 %fusion = f32[4,16,128,128]{3,2,1,0:T(8,128)} fusion(bf16[4,128,128,1]{2,1,3,0:T(8,128)(2,1)S(1)} %bitcast.62, bf16[4,16,128,256]{3,2,1,0:T(8,128)(2,1)} %bitcast.65, bf16[4,128,256,1]{2,1,3,0:T(8,128)(2,1)S(1)} %bitcast.67, f32[4,128]{1,0:T(4,128)S(1)} %bitcast.68, f32[4,16,128]{2,1,0:T(8,128)S(1)} %multiply_reduce_fusion), kind=kOutput, calls=%fused_computation.4 | convolution fusion | flops 811597824 | bytes 8816640 | tf_op jit(solution)/shard_map/jtab,jbv->jtav/dot_general | solution.py:51
  85.4 2.5 %broadcast_in_dim.4 = f32[64,128,128]{2,1,0:T(8,128)} broadcast(f32[]{:T(128)} %constant.43.clone.1), dimensions={} | broadcast | bytes 4194308 | tf_op jit(solution)/shard_map/broadcast_in_dim | solution.py:52
  87.9 13.6 %scatter_fusion = f32[64,128,128]{2,1,0:T(8,128)} fusion(f32[64,128,128]{2,1,0:T(8,128)} %broadcast_in_dim.4, s32[64]{0:T(128)S(1)} %fusion.15, f32[64,128,128]{2,1,0:T(8,128)} %bitcast.66), kind=kCustom, calls=%fused_computation.1 | custom fusion | flops 1048576 | bytes 12583168 | tf_op jit(solution)/shard_map/scatter-add | solution.py:53
  101.6 0.7 copy-done.2
  103.4 5.8 %cholesky.59 = f32[64,64]{1,0:T(8,128)S(1)} custom-call(f32[64,64]{1,0:T(8,128)S(1)} %fusion.9), custom_call_target="Cholesky" | custom-call | tf_op jit(solution)/shard_map/jit(cholesky)/cholesky | solution.py:59
  109.2 0.6 compare_reduce_fusion.2
  109.9 0.7 fusion.10
  110.5 1.9 collective-permute-start
  112.7 1.0 collective-permute-done
  113.9 5.8 %cholesky.70 = f32[64,64]{1,0:T(8,128)S(1)} custom-call(f32[64,64]{1,0:T(8,128)S(1)} %fusion.8), custom_call_target="Cholesky" | custom-call | tf_op jit(solution)/shard_map/jit(cholesky)/cholesky | solution.py:29
  120.5 0.7 select_bitcast_fusion.1
  121.1 8.7 %collective-permute-start.1 = (f32[64,64]{1,0:T(8,128)S(1)}, f32[64,64]{1,0:T(8,128)S(1)}, u32[]{:S(2)}, u32[]{:S(2)}) collective-permute-start(f32[64,64]{1,0:T(8,128)S(1)} %get-tuple-element.9), channel_id=1, source_target_pairs={{0,2},{1,3},{2,0},{3,1},{4,6},{5,7},{6,4},{7,5},{8,10},{9,11},{10,... | collective-permute-start | bytes 49160 | tf_op jit(solution)/shard_map/ppermute | solution.py:14
  129.9 4.9 %custom-call.6 = f32[1,64,64]{1,2,0:T(8,128)S(1)} custom-call(f32[1,64,64]{2,1,0:T(8,128)S(1)} %get-tuple-element.8), custom_call_target="InvertDiagBlocksLowerTriangular" | custom-call | tf_op jit(solution)/shard_map/triangular_solve/custom-call.0 | solution.py:30
  135.5 5.8 %cholesky.81 = f32[64,64]{1,0:T(8,128)S(1)} custom-call(f32[64,64]{1,0:T(8,128)S(1)} %fusion.6), custom_call_target="Cholesky" | custom-call | tf_op jit(solution)/shard_map/jit(cholesky)/cholesky | solution.py:29
  142.0 0.7 select_bitcast_fusion
  142.7 4.9 %custom-call.7 = f32[1,64,64]{1,2,0:T(8,128)S(1)} custom-call(f32[1,64,64]{2,1,0:T(8,128)S(1)} %get-tuple-element.12), custom_call_target="InvertDiagBlocksLowerTriangular" | custom-call | tf_op jit(solution)/shard_map/triangular_solve/custom-call.0 | solution.py:30
  147.9 0.7 copy.25
  148.6 56.8 %reduce-scatter.2.cloned.1.call-done = f32[512,128]{1,0:T(8,128)} async-done(((f32[8192,128]{1,0:T(8,128)}), f32[512,128]{1,0:T(8,128)}) %reduce-scatter.2.cloned.1.call-update) | async-done | bytes 262160 | tf_op jit(solution)/shard_map/reduce_scatter | solution.py:54
  205.4 1.6 convert_element_type.20
  (37 shorter events, 4.2 us)
Async XLA Ops:
  7.2 73.4 %copy-start = (bf16[512,128]{1,0:T(8,128)(2,1)S(1)}, bf16[512,128]{1,0:T(8,128)(2,1)}, u32[]{:S(2)}) copy-start(bf16[512,128]{1,0:T(8,128)(2,1)} %param.8) | copy-start | bytes 393220
  10.5 10.4 %copy-start.3 = (s32[4,16]{1,0:T(4,128)S(1)}, s32[4,16]{1,0:T(4,128)}, u32[]{:S(2)}) copy-start(s32[4,16]{1,0:T(4,128)} %param.9) | copy-start | bytes 772
  10.5 10.5 %copy-start.1 = (bf16[512,256]{1,0:T(8,128)(2,1)S(1)}, bf16[512,256]{1,0:T(8,128)(2,1)}, u32[]{:S(2)}) copy-start(bf16[512,256]{1,0:T(8,128)(2,1)} %param.7) | copy-start | bytes 786436
  10.5 61.7 %all-to-all-start = ((bf16[16,512,256]{2,1,0:T(8,128)(2,1)}), bf16[16,512,256]{2,1,0:T(8,128)(2,1)}, u32[]{:S(2)}, u32[]{:S(2)}) async-start(bf16[16,512,256]{2,1,0:T(8,128)(2,1)} %stack.2), calls=%async_computation | async-start | bytes 8388608 | tf_op jit(solution)/shard_map/all_to_all | solution.py:39
  20.8 184.5 %reduce-scatter.2.cloned.1.call-start = ((), (), s32[]{:S(2)}) async-start(), calls=%async_computation.2 | async-start | bytes 4456448 | tf_op jit(solution)/shard_map/reduce_scatter | solution.py:54
  101.6 0.8 copy-start.2
  110.5 3.1 %collective-permute-start = (f32[64,64]{1,0:T(8,128)S(1)}, f32[64,64]{1,0:T(8,128)S(1)}, u32[]{:S(2)}, u32[]{:S(2)}) collective-permute-start(f32[64,64]{1,0:T(8,128)S(1)} %fusion.10), channel_id=1, source_target_pairs={{0,1},{1,0},{2,3},{3,2},{4,5},{5,4},{6,7},{7,6},{8,9},{9,8},{10,11... | collective-permute-start | bytes 49160 | tf_op jit(solution)/shard_map/ppermute | solution.py:14
  121.1 14.1 %collective-permute-start.1 = (f32[64,64]{1,0:T(8,128)S(1)}, f32[64,64]{1,0:T(8,128)S(1)}, u32[]{:S(2)}, u32[]{:S(2)}) collective-permute-start(f32[64,64]{1,0:T(8,128)S(1)} %get-tuple-element.9), channel_id=1, source_target_pairs={{0,2},{1,3},{2,0},{3,1},{4,6},{5,7},{6,4},{7,5},{8,10},{9,11},{10,... | collective-permute-start | bytes 49160 | tf_op jit(solution)/shard_map/ppermute | solution.py:14
Sparse Core Ops, SparseCore 0:
  101.7 103.6 reduce-scatter.1
